TPU v7x, 32 devices: a whole 2x2x4 slice. The times are simulated.
32 devices in a mesh: groups: 2 (over x), sub: 16 (over z, y, core).
Axes of the slice: x: 2, y: 2, z: 4, core: 2. Of those that a mesh axis runs over, the one named last changes fastest.
Arguments:
- rhs: float32 [32, 196608], P('groups', 'sub'), parts along dimension 0, may hold values from -8 to 8
- mass: float32 [393216], P(('groups', 'sub')), parts along dimension 0, may hold values from 0.5 to 2
- jacobi: float32 [393216], P(('groups', 'sub')), parts along dimension 0, may hold values from 0.1 to 1
- local_edges: int32 [2, 12288], P(None, ('groups', 'sub')), parts along dimension 1, may hold values from 0 to 191, as said below
- local_blocks: float32 [64, 786432], P(None, ('groups', 'sub')), parts along dimension 1, may hold values from -0.75 to 0.75
- if_rows: int32 [1024], P(('groups', 'sub')), parts along dimension 0, may hold values from 0 to 191
- send_rows: int32 [1024], P(('groups', 'sub')), parts along dimension 0, may hold values from 0 to 191
- if_count: int32 [32], P(('groups', 'sub')), parts along dimension 0, may hold values from 1 to 32, as said below
- if_blocks: float32 [64, 65536], P(None, ('groups', 'sub')), parts along dimension 1, may hold values from -0.75 to 0.75
- coarse_basis: float32 [64, 393216], P(None, ('groups', 'sub')), parts along dimension 1, may hold values from -0.109375 to 0.109375
- coarse_factor: float32 [2048, 1024], P(('groups', 'sub')), parts along dimension 0, may hold values from -0.1875 to 0.1875
Outputs:
- solution: float32 [32, 196608], P('groups', 'sub'), parts along dimension 0
- precond_residual: float32 [32, 196608], P('groups', 'sub'), parts along dimension 0
There are 2 independent parts, one for each index of `groups`. A program takes and returns all parts, laid end to end along the dimension named above; each array names one. Nothing has to cross between parts.
Inputs may be any that keep to these rules, and one draw needn't show every extreme that they name: `local_edges`: the two rows of each element differ. `if_count`: some subdomain has exactly 32 live slots in every draw.
All inputs are finite; a program needn't handle non-finite values.
Results may differ from a plain program's by a relative error of at most 0.0003.
Values sent between devices are 32-bit elements; how exact they have to be, the bound alone decides.
A program may use at most 128 MiB of HBM per device.

v0:
```python
import jax
import jax.numpy as jnp
from jax import lax
from jax.sharding import PartitionSpec as P

ITERS = 2


HIGH = lax.Precision.HIGHEST


def shifted(value, axis, steps):
    count = lax.axis_size(axis)
    pairs = [(source, (source + steps) % count) for source in range(count)]
    return lax.ppermute(value, axis, pairs)


def one_hot(index, width):
    return (index[:, None] == jnp.arange(width, dtype=jnp.int32)[None, :]).astype(jnp.float32)


def element_force(diff, blocks):
    strain = jnp.einsum("rek,kej->rej", diff, blocks, precision=HIGH)
    return jnp.einsum("rej,kej->rek", strain, blocks, precision=HIGH)


def spread_rows(mapping, force):
    return jnp.einsum("en,rek->rnk", mapping, force, precision=HIGH)


def load_sums(left, right):
    return lax.psum(jnp.sum(left * right, axis=1), "sub")


def body(
    rhs,
    mass,
    jacobi,
    local_edges,
    local_blocks,
    if_rows,
    send_rows,
    if_count,
    if_blocks,
    coarse_basis,
    coarse_factor,
):
    loads, width = rhs.shape
    block = local_blocks.shape[0]
    rows = width // block
    edge_count = local_edges.shape[1]
    slots = if_rows.shape[0]
    blocks = local_blocks.reshape(block, edge_count, block)
    iface = if_blocks.reshape(block, slots, block)
    incidence = one_hot(local_edges[0], rows) - one_hot(local_edges[1], rows)
    own_map = one_hot(if_rows, rows)
    live = (jnp.arange(slots, dtype=jnp.int32) < if_count[0]).astype(jnp.float32)
    mass_rows = mass.reshape(rows, block)

    def precondition(residual):
        coarse = lax.dot_general(residual, coarse_basis, (((1,), (1,)), ((), ())), precision=HIGH)
        partial_value = jnp.dot(coarse, coarse_factor, precision=HIGH)
        whole_w = lax.psum(partial_value, "sub")
        gamma = jnp.zeros((loads,), jnp.float32)
        own_coef = lax.dot_general(whole_w, coarse_factor, (((1,), (1,)), ((), ())), precision=HIGH)
        result = residual * jacobi[None, :] + jnp.dot(own_coef, coarse_basis, precision=HIGH)
        return (result, gamma)

    solution = jnp.zeros_like(rhs)
    residual = rhs
    precond, gamma = precondition(residual)
    gamma = load_sums(residual, precond)
    direction = precond
    for step in range(ITERS):
        field = direction.reshape(loads, rows, block)
        remote_all, remote_index = shifted((field, send_rows.astype(jnp.float32)), "sub", -1)
        remote_rows = remote_index.astype(jnp.int32)
        remote = remote_all[:, remote_rows, :]
        local_force = element_force(field[:, local_edges[0]] - field[:, local_edges[1]], blocks)
        total = mass_rows[None] * field + spread_rows(incidence, local_force)
        iface_force = element_force(field[:, if_rows] - remote, iface) * live[None, :, None]
        total = total + spread_rows(own_map, iface_force)
        laid_out = spread_rows(one_hot(remote_rows, rows), iface_force)
        total = total - shifted(laid_out, "sub", 1)
        image = total.reshape(loads, width)
        alpha = gamma / lax.psum(jnp.sum(direction * image, axis=1), "sub")
        solution = solution + alpha[:, None] * direction
        residual = residual - alpha[:, None] * image
        precond, gamma_next = precondition(residual)
        if step + 1 < ITERS:
            gamma_next = load_sums(residual, precond)
            direction = precond + (gamma_next / gamma)[:, None] * direction
            gamma = gamma_next
    return (solution, precond)


def solution(mesh):
    in_specs = (
        P("groups", "sub"),
        P(("groups", "sub")),
        P(("groups", "sub")),
        P(None, ("groups", "sub")),
        P(None, ("groups", "sub")),
        P(("groups", "sub")),
        P(("groups", "sub")),
        P(("groups", "sub")),
        P(None, ("groups", "sub")),
        P(None, ("groups", "sub")),
        P(("groups", "sub"), None),
    )
    out_specs = (P("groups", "sub"), P("groups", "sub"))
    return jax.shard_map(body, mesh=mesh, in_specs=in_specs, out_specs=out_specs, check_vma=False)
```

profile of v0, /device:TPU:0, one launch (start us, length us, event | category | flops | bytes accessed | tf_op | source)
XLA Modules:
  0.0 608.4 jit_solution(5660781528087845299)
XLA Ops:
  8.6 5.4 collective-permute-start.1
  14.1 3.7 fusion.77
  21.2 2.5 reshape.94
  23.7 10.9 %reshape.93 = f32[64,384,64]{2,1,0:T(8,128)} reshape(f32[64,24576]{1,0:T(8,128)} %param.15) | data formatting | bytes 12582912 | tf_op jit(solution)/shard_map/reshape | solution.py:53
  36.3 64.7 %all-reduce.5.cloned.1.call-done = f32[16,1024]{1,0:T(8,128)} async-done(((f32[16,1024]{1,0:T(8,128)}), f32[16,1024]{1,0:T(8,128)}) %all-reduce.5.cloned.1.call-update) | async-done | bytes 65552 | tf_op jit(solution)/shard_map/psum | solution.py:63
  102.1 3.6 convolution_add_fusion.2
  105.7 2.9 reshape.92
  108.7 3.0 copy.43
  111.6 3.5 copy.44
  115.2 2.4 collective-permute-start
  117.6 2.7 gather_fusion.2
  120.3 4.0 gather_fusion.1
  124.2 3.9 gather_fusion
  128.2 23.1 %fusion.6 = f32[384,16,64]{2,1,0:T(8,128)} fusion(f32[64,384,64]{2,1,0:T(8,128)} %reshape.93, f32[384,16,64]{2,1,0:T(8,128)} %gather_fusion, f32[384,16,64]{2,1,0:T(8,128)} %gather_fusion.1), kind=kOutput, calls=%fused_computation.17 | convolution fusion | flops 302383104 | bytes 11010048 | tf_op jit(solution)/shard_map/rek,kej->rej/dot_general | solution.py:23
  151.3 3.1 copy.51
  154.4 2.7 gather_fusion.3
  157.1 3.1 convolution_bitcast_fusion.5
  160.1 3.4 fusion.45
  165.2 29.4 %fusion.18 = f32[16,384,64]{2,0,1:T(8,128)S(1)} fusion(f32[64,384,64]{2,1,0:T(8,128)} %reshape.93, f32[384,16,64]{2,1,0:T(8,128)S(1)} %copy-done.3), kind=kOutput, calls=%fused_computation.29 | convolution fusion | flops 301989888 | bytes 9437184 | tf_op jit(solution)/shard_map/rej,kej->rek/dot_general | solution.py:24
  194.6 6.6 %fusion.35 = f32[16,192,64]{1,2,0:T(8,128)S(1)} fusion(f32[16,384,64]{2,0,1:T(8,128)S(1)} %fusion.18, f32[16,192,64]{1,2,0:T(8,128)} %copy.43, f32[192,64]{0,1:T(8,128)S(1)} %copy.42, s32[384]{0:T(512)S(1)} %get-tuple-element.5, s32[384]{0:T(512)S(1)} %get-tuple-element.4), kind=kOutput, calls=%fused_computation.40 | convolution fusion | flops 906731520 | bytes 3197952 | tf_op jit(solution)/shard_map/en,rek->rnk/dot_general | solution.py:28
  203.0 2.9 copy.56
  205.9 2.8 reshape.95
  208.7 2.4 multiply_reduce_fusion.2
  211.1 34.6 %all-reduce = (f32[16]{0:T(128)}, f32[16]{0:T(128)}) all-reduce(f32[16]{0:T(128)} %get-tuple-element.3, f32[16]{0:T(128)} %get-tuple-element.2), channel_id=1, replica_groups=mesh['groups'=2,'sub'=16] {'sub'}, use_global_device_ids=true, to_apply=%region_2.0 | all-reduce | flops 32 | bytes 256 | tf_op jit(solution)/shard_map/psum | solution.py:32
  249.5 2.6 fusion.80
  253.0 81.8 %all-reduce.7.cloned.1.call-done = f32[16,1024]{1,0:T(8,128)} async-done(((f32[16,1024]{1,0:T(8,128)}), f32[16,1024]{1,0:T(8,128)}) %all-reduce.7.cloned.1.call-update) | async-done | bytes 65552 | tf_op jit(solution)/shard_map/psum | solution.py:63
  335.9 4.3 multiply_reduce_fusion.1
  340.2 32.6 %psum.53 = f32[16]{0:T(128)} all-reduce(f32[16]{0:T(128)} %get-tuple-element.10), channel_id=1, replica_groups=mesh['groups'=2,'sub'=16] {'sub'}, use_global_device_ids=true, to_apply=%region_7.0 | all-reduce | flops 16 | bytes 128 | tf_op jit(solution)/shard_map/psum | solution.py:32
  375.9 2.9 reshape.96
  378.8 3.0 copy.57
  381.8 3.5 copy.58
  385.3 2.7 gather_fusion.6
  388.0 4.0 gather_fusion.5
  392.0 3.9 gather_fusion.4
  395.9 23.1 %fusion.2 = f32[384,16,64]{2,1,0:T(8,128)} fusion(f32[64,384,64]{2,1,0:T(8,128)} %reshape.93, f32[384,16,64]{2,1,0:T(8,128)} %gather_fusion.4, f32[384,16,64]{2,1,0:T(8,128)} %gather_fusion.5), kind=kOutput, calls=%fused_computation.13 | convolution fusion | flops 302383104 | bytes 11010048 | tf_op jit(solution)/shard_map/rek,kej->rej/dot_general | solution.py:23
  419.0 3.1 copy.65
  422.1 2.7 gather_fusion.7
  424.8 3.1 convolution_bitcast_fusion.4
  427.9 3.4 fusion.44
  432.5 29.5 %fusion.23 = f32[16,384,64]{2,0,1:T(8,128)S(1)} fusion(f32[64,384,64]{2,1,0:T(8,128)} %reshape.93, f32[384,16,64]{2,1,0:T(8,128)S(1)} %copy-done.2), kind=kOutput, calls=%fused_computation.30 | convolution fusion | flops 301989888 | bytes 9437184 | tf_op jit(solution)/shard_map/rej,kej->rek/dot_general | solution.py:24
  462.0 5.4 fusion.41
  469.1 2.9 copy.70
  471.9 2.8 reshape.97
  476.3 33.4 %psum.54 = f32[16]{0:T(128)S(1)} all-reduce(f32[16]{0:T(128)S(1)} %multiply_reduce_fusion), channel_id=1, replica_groups=mesh['groups'=2,'sub'=16] {'sub'}, use_global_device_ids=true, to_apply=%region_9.0 | all-reduce | flops 16 | bytes 128 | tf_op jit(solution)/shard_map/psum | solution.py:86
  509.7 4.0 fusion.64
  514.6 2.4 multiply_add_fusion
  517.0 79.4 %all-reduce.9.cloned.1.call-done = f32[16,1024]{1,0:T(8,128)} async-done(((f32[16,1024]{1,0:T(8,128)}), f32[16,1024]{1,0:T(8,128)}) %all-reduce.9.cloned.1.call-update) | async-done | bytes 65552 | tf_op jit(solution)/shard_map/psum | solution.py:63
  597.6 3.9 convolution_add_fusion
  (72 shorter events, 25.6 us)
Async XLA Ops:
  7.2 6.9 %copy-start = (f32[64,12288]{1,0:T(8,128)S(1)}, f32[64,12288]{1,0:T(8,128)}, u32[]{:S(2)}) copy-start(f32[64,12288]{1,0:T(8,128)} %param.20) | copy-start | bytes 9437188
  7.2 10.6 %copy-start.4 = (f32[64,1024]{1,0:T(8,128)S(1)}, f32[64,1024]{1,0:T(8,128)}, u32[]{:S(2)}) copy-start(f32[64,1024]{1,0:T(8,128)} %param.21) | copy-start | bytes 786436
  7.2 11.5 %copy-start.8 = (s32[2,384]{1,0:T(2,128)S(1)}, s32[2,384]{1,0:T(2,128)}, u32[]{:S(2)}) copy-start(s32[2,384]{1,0:T(2,128)} %param.14) | copy-start | bytes 9220
  7.2 12.2 %copy-start.9 = (s32[32]{0:T(128)S(1)}, s32[32]{0:T(128)}, u32[]{:S(2)}) copy-start(s32[32]{0:T(128)} %param.16) | copy-start | bytes 388
  7.2 12.3 %copy-start.7 = (f32[12288]{0:T(1024)S(1)}, f32[12288]{0:T(1024)}, u32[]{:S(2)}) copy-start(f32[12288]{0:T(1024)} %param.12) | copy-start | bytes 147460
  7.2 93.8 %all-reduce.5.cloned.1.call-start = ((), (), s32[]{:S(2)}) async-start(), calls=%async_computation | async-start | bytes 131072 | tf_op jit(solution)/shard_map/psum | solution.py:63
  8.6 25.9 %collective-permute-start.1 = (f32[32]{0:T(128)}, f32[32]{0:T(128)S(1)}, u32[]{:S(2)}, u32[]{:S(2)}) collective-permute-start(f32[32]{0:T(128)} %convert_element_type.26), channel_id=1, source_target_pairs={{0,15},{1,0},{2,1},{3,2},{4,3},{5,4},{6,5},{7,6},{8,7},{9,8},{10,9... | collective-permute-start | bytes 392 | tf_op jit(solution)/shard_map/ppermute | solution.py:15
  18.7 316.2 %all-reduce.7.cloned.1.call-start = ((), (), s32[]{:S(2)}) async-start(), calls=%async_computation.1 | async-start | bytes 131072 | tf_op jit(solution)/shard_map/psum | solution.py:63
  23.7 78.4 %copy-start.6 = (f32[12288]{0:T(1024)S(1)}, f32[12288]{0:T(1024)}, u32[]{:S(2)}) copy-start(f32[12288]{0:T(1024)} %param.13) | copy-start | bytes 147460
  34.5 0.5 copy-start.13
  115.2 36.1 %collective-permute-start = (f32[16,192,64]{1,2,0:T(8,128)}, f32[16,192,64]{1,2,0:T(8,128)}, u32[]{:S(2)}, u32[]{:S(2)}) collective-permute-start(f32[16,192,64]{1,2,0:T(8,128)} %copy.43), channel_id=1, source_target_pairs={{0,15},{1,0},{2,1},{3,2},{4,3},{5,4},{6,5},{7,6},{8,7},{9,8},{10,9... | collective-permute-start | bytes 2359304 | tf_op jit(solution)/shard_map/ppermute | solution.py:15
  157.1 8.1 %copy-start.3 = (f32[384,16,64]{2,1,0:T(8,128)S(1)}, f32[384,16,64]{2,1,0:T(8,128)}, u32[]{:S(2)}) copy-start(f32[384,16,64]{2,1,0:T(8,128)} %fusion.6) | copy-start | bytes 4718596
  164.9 36.4 %collective-permute-start.2 = (f32[16,192,64]{1,2,0:T(8,128)S(1)}, f32[16,192,64]{1,2,0:T(8,128)S(1)}, u32[]{:S(2)}, u32[]{:S(2)}) collective-permute-start(f32[16,192,64]{1,2,0:T(8,128)S(1)} %convolution_bitcast_fusion.2), channel_id=1, source_target_pairs={{0,1},{1,2},{2,3},{3,4},{4,5},{5,6},{6,7},{7,8},{8,9},{9,10},{10,1... | collective-permute-start | bytes 2359304 | tf_op jit(solution)/shard_map/ppermute | solution.py:15
  246.4 0.6 copy-start.11
  248.5 0.9 copy-start.1
  252.9 343.5 %all-reduce.9.cloned.1.call-start = ((), (), s32[]{:S(2)}) async-start(), calls=%async_computation.2 | async-start | bytes 131072 | tf_op jit(solution)/shard_map/psum | solution.py:63
  395.9 23.1 %collective-permute-start.3 = (f32[16,192,64]{1,2,0:T(8,128)}, f32[16,192,64]{1,2,0:T(8,128)}, u32[]{:S(2)}, u32[]{:S(2)}) collective-permute-start(f32[16,192,64]{1,2,0:T(8,128)} %copy.57), channel_id=1, source_target_pairs={{0,15},{1,0},{2,1},{3,2},{4,3},{5,4},{6,5},{7,6},{8,7},{9,8},{10,9... | collective-permute-start | bytes 2359304 | tf_op jit(solution)/shard_map/ppermute | solution.py:15
  419.0 12.3 %copy-start.10 = (s32[32]{0:T(128)S(1)}, s32[32]{0:T(128)}, u32[]{:S(2)}) copy-start(s32[32]{0:T(128)} %convert_element_type.27) | copy-start | bytes 388
  424.8 7.7 %copy-start.2 = (f32[384,16,64]{2,1,0:T(8,128)S(1)}, f32[384,16,64]{2,1,0:T(8,128)}, u32[]{:S(2)}) copy-start(f32[384,16,64]{2,1,0:T(8,128)} %fusion.2) | copy-start | bytes 4718596
  432.0 30.0 %copy-start.5 = (f32[16,192,64]{1,2,0:T(8,128)S(1)}, f32[16,192,64]{1,2,0:T(8,128)}, u32[]{:S(2)}) copy-start(f32[16,192,64]{1,2,0:T(8,128)} %copy.57) | copy-start | bytes 2359300
  432.0 35.5 %collective-permute-start.4 = (f32[16,192,64]{1,2,0:T(8,128)S(1)}, f32[16,192,64]{1,2,0:T(8,128)S(1)}, u32[]{:S(2)}, u32[]{:S(2)}) collective-permute-start(f32[16,192,64]{1,2,0:T(8,128)S(1)} %convolution_bitcast_fusion), channel_id=1, source_target_pairs={{0,1},{1,2},{2,3},{3,4},{4,5},{5,6},{6,7},{7,8},{8,9},{9,10},{10,1... | collective-permute-start | bytes 2359304 | tf_op jit(solution)/shard_map/ppermute | solution.py:15
  469.1 40.7 %copy-start.14 = (f32[16]{0:T(128)S(1)}, f32[16]{0:T(128)}, u32[]{:S(2)}) copy-start(f32[16]{0:T(128)} %psum.53) | copy-start | bytes 196
  474.7 39.9 %copy-start.12 = (f32[16]{0:T(128)S(1)}, f32[16]{0:T(128)}, u32[]{:S(2)}) copy-start(f32[16]{0:T(128)} %copy-done.11) | copy-start | bytes 196
Sparse Core Ops, SparseCore 0:
  18.8 82.1 all-reduce.4
  253.1 81.7 all-reduce.6
  514.7 81.6 all-reduce.8
where the time goes:
time: 617 us; the launch traced here: 608 us
  waiting for transfers between devices  226 us (37%)
  matrix products  163 us (26%)
  blocking collectives  101 us (16%)
  local copies, waits for them, and re-layouts  80 us (13%)
  between operations  15.2 us (2%)
  other arithmetic  14.4 us (2%)
  starting transfers between devices  8.83 us (1%)
    psum x3, waiting for transfers between devices, precondition(): whole_w = lax.psum(partial_value, 'sub')  226 us
    psum x2, blocking collectives, load_sums(): return lax.psum(jnp.sum(left * right, axis=1), 'sub')  67.2 us
    dot_general x4, matrix products, element_force(): return jnp.einsum('rej,kej->rek', strain, blocks, precision=HIGH)  65.7 us
    dot_general x4, matrix products, element_force(): strain = jnp.einsum('rek,kej->rej', diff, blocks, precision=HIGH)  52.4 us
    psum x1, blocking collectives, body(): alpha = gamma / lax.psum(jnp.sum(direction * image, axis=1), 'sub')  33.4 us
    reshape x6, local copies, waits for them, and re-layouts, body(): field = direction.reshape(loads, rows, block)  18.8 us
    dot_general x6, matrix products, spread_rows(): return jnp.einsum('en,rek->rnk', mapping, force, precision=HIGH)  17.3 us
  transfers between devices with their start and end apart: 8, of which 3 were waited for; matrix products, arithmetic and copies ran while one was open for 25% of the time, Pallas kernels for 0%

commit v1 on v0

v1 whole, which is shorter than its diff:
```python
import functools

import jax
import jax.numpy as jnp
from jax import lax
from jax.experimental import pallas as pl
from jax.experimental.pallas import tpu as pltpu
from jax.sharding import PartitionSpec as P

ITERS = 2
F32 = jnp.float32
BF16 = jnp.bfloat16
MESH = pl.DeviceIdType.MESH


def split(x):
    high = x.astype(BF16)
    return high, (x - high.astype(F32)).astype(BF16)


def stacked(x):
    high, low = split(x)
    return jnp.concatenate([high, low], axis=0)


def dot(a, b):
    return jnp.dot(a, b, preferred_element_type=F32)


def dot_t(a, b):
    return lax.dot_general(a, b, (((1,), (1,)), ((), ())), preferred_element_type=F32)


def fold(o, rows):
    a = o[:rows] + o[rows:]
    return a + pltpu.roll(a, 64, 1)


def kernel(
    n,
    mass_ref,
    jac_ref,
    edges_s,
    ifr_s,
    snd_s,
    cnt_s,
    edges_v,
    ifr_v,
    snd_v,
    rhs_h,
    blocks_h,
    ifb_h,
    basis_h,
    fac_h,
    x_ref,
    z_ref,
    r_ref,
    p_ref,
    q_ref,
    v_ref,
    qrow_ref,
    t_ref,
    inc_ref,
    stage_ref,
    basis_st,
    fac_st,
    bb_ref,
    bs_ref,
    ff_ref,
    w_ref,
    pw_ref,
    msg_a,
    rcv_a,
    msg_b,
    rcv_b,
    halo_s,
    halo_r,
    frc_s,
    frc_r,
    in_sem,
    sa_sem,
    ra_sem,
    sb_sem,
    rb_sem,
    sh_sem,
    rh_sem,
    sf_sem,
    rf_sem,
):
    loads, width = rhs_h.shape
    rows = width // 64
    ne = edges_v.shape[1]
    slots = ifr_v.shape[1]
    nc = fac_h.shape[1]
    wide_e = t_ref.shape[0] // loads
    me = lax.axis_index("sub")
    nxt = lax.rem(me + 1, n)
    prv = lax.rem(me + n - 1, n)
    lcols = ne * 64

    cp_rhs = pltpu.make_async_copy(rhs_h, r_ref, in_sem.at[0])
    cp_basis = pltpu.make_async_copy(basis_h, basis_st, in_sem.at[1])
    cp_fac = pltpu.make_async_copy(fac_h, fac_st, in_sem.at[2])
    cp_blk = pltpu.make_async_copy(blocks_h, stage_ref.at[:, pl.ds(0, lcols)], in_sem.at[3])
    cp_ifb = pltpu.make_async_copy(ifb_h, stage_ref.at[:, pl.ds(lcols, slots * 64)], in_sem.at[4])
    for cp in (cp_rhs, cp_basis, cp_fac, cp_blk, cp_ifb):
        cp.start()

    barrier = pltpu.get_barrier_semaphore()

    @pl.loop(1, n)
    def _(k):
        pl.semaphore_signal(barrier, inc=1, device_id={"sub": lax.rem(me + k, n)}, device_id_type=MESH)

    low_half = lax.broadcasted_iota(jnp.int32, (loads, 128), 1) < 64
    low_half8 = lax.broadcasted_iota(jnp.int32, (8, 128), 1) < 64
    low_half64 = lax.broadcasted_iota(jnp.int32, (64, 128), 1) < 64
    own_block = (lax.broadcasted_iota(jnp.int32, (64, 256), 0) >> 4) == (lax.broadcasted_iota(jnp.int32, (64, 256), 1) >> 6)

    def lanes(i, size):
        return pl.ds(pl.multiple_of(i * size, size), size)

    def pack16(s):
        return jnp.where(low_half8, s[:8], s[8:])

    def unpack16(t):
        return jnp.concatenate([jnp.broadcast_to(t[:, 0:1], (8, 128)), jnp.broadcast_to(t[:, 64:65], (8, 128))], axis=0)

    def bcast(s):
        return jnp.broadcast_to(jnp.sum(s, axis=1, keepdims=True), (loads, 128))

    def split_into(src, dst, total, size):
        @pl.loop(0, total // size)
        def _(i):
            dst[:, lanes(i, size)] = stacked(src[:, lanes(i, size)])

    def contract(src, mat, total, size):
        def step(i, o):
            return o + dot_t(stacked(src[:, lanes(i, size)]), mat[:, lanes(i, size)])
        o = lax.fori_loop(0, total // size, step, jnp.zeros((2 * loads, 128), F32))
        return fold(o, loads)

    def send_parts(phase, coarse, scalars):
        lhs = stacked(coarse)

        @pl.loop(0, nc // 512)
        def _(i):
            o = dot(lhs, ff_ref[:, lanes(i, 512)])
            o = o[:loads] + o[loads:]
            for c in range(4):
                for h in range(2):
                    msg_a[phase, 8 * i + 2 * c + h, 0:8] = o[8 * h : 8 * h + 8, 128 * c : 128 * c + 128]
                    msg_a[phase, 8 * i + 2 * c + h, 8:16] = scalars

        rcv_a[phase, me] = msg_a[phase, me]

        @pl.loop(1, n)
        def _(k):
            to = lax.rem(me + k, n)
            pltpu.make_async_remote_copy(
                msg_a.at[phase, to], rcv_a.at[phase, me], sa_sem.at[phase], ra_sem.at[phase],
                device_id={"sub": to}, device_id_type=MESH,
            ).start()

    def wait_all(buf, phase, sem):
        part = buf.at[phase, pl.ds(0, n - 1)]
        pltpu.make_async_copy(part, part, sem.at[phase]).wait()

    def take_parts(phase):
        wait_all(rcv_a, phase, ra_sem)
        s = lax.fori_loop(0, n, lambda j, s: s + rcv_a[phase, j], jnp.zeros((16, 128), F32))
        return s[:8], unpack16(s[8:])

    def send_whole(phase, tile, scalars):
        both = jnp.concatenate([tile, scalars], axis=0)
        msg_b[phase] = both
        rcv_b[phase, me] = both

        @pl.loop(1, n)
        def _(k):
            to = lax.rem(me + k, n)
            pltpu.make_async_remote_copy(
                msg_b.at[phase], rcv_b.at[phase, me], sb_sem.at[phase], rb_sem.at[phase],
                device_id={"sub": to}, device_id_type=MESH,
            ).start()

    def take_whole(phase, alpha):
        wait_all(rcv_b, phase, rb_sem)

        def step(m, carry):
            norm, s = carry
            first = rcv_b[phase, 2 * m]
            second = rcv_b[phase, 2 * m + 1]
            w = jnp.concatenate([first[:8], second[:8]], axis=0)
            if alpha is not None:
                w = w_ref[:, lanes(m, 128)] - alpha * w
            w_ref[:, lanes(m, 128)] = w
            return norm + w * w, s + first[8:] + second[8:]

        norm, s = lax.fori_loop(0, n // 2, step, (jnp.zeros((loads, 128), F32), jnp.zeros((8, 128), F32)))
        return bcast(norm) + unpack16(s)

    def weighted(scale_ref, src):
        def step(i, s):
            v = src[:, lanes(i, 512)]
            v = scale_ref[:, lanes(i, 512)] * v * v
            return s + v[:, :128] + v[:, 128:256] + v[:, 256:384] + v[:, 384:]
        return lax.fori_loop(0, width // 512, step, jnp.zeros((loads, 128), F32))

    def precondition(visit):
        lhs = stacked(contract(w_ref, ff_ref, nc, 512))

        @pl.loop(0, width // 512)
        def _(i):
            o = dot(lhs, bs_ref[:, lanes(i, 512)])
            visit(i, jac_ref[:, lanes(i, 512)] * r_ref[:, lanes(i, 512)] + o[:loads] + o[loads:])

    def set_direction(i, p):
        p_ref[:, lanes(i, 512)] = p
        for c in range(4):
            a = p[:, 128 * c : 128 * c + 128]
            b = pltpu.roll(a, 64, 1)
            v_ref[8 * i + 2 * c] = jnp.where(low_half, a, b)
            v_ref[8 * i + 2 * c + 1] = jnp.where(low_half, b, a)

    def put_force(row, t):
        high = t.astype(BF16).astype(F32)
        t_ref[pl.ds(pl.multiple_of(row * loads, 16), t.shape[0]), :] = jnp.where(
            low_half64 if t.shape[0] == 64 else low_half, high, t - high
        )

    def force(d, col):
        b = bb_ref[:, pl.ds(pl.multiple_of(col, 256), 256)]
        u = dot(stacked(d), b)
        u = jnp.where(own_block, u[:64] + u[64:], 0.0)
        t = fold(dot_t(stacked(u), b), 64)
        u2 = u * u
        return t, u2[0:16] + u2[16:32] + u2[32:48] + u2[48:64]

    def local_groups(start, stop, acc):
        def step(g, acc):
            d = jnp.concatenate([v_ref[edges_s[0, 4 * g + k]] - v_ref[edges_s[1, 4 * g + k]] for k in range(4)], axis=0)
            t, e = force(d, 256 * g)
            put_force(4 * g, t)
            return acc + e
        return lax.fori_loop(start, stop, step, acc)

    cp_rhs.wait()
    cp_basis.wait()
    split_into(basis_st, bs_ref, width, 512)
    coarse = contract(r_ref, bs_ref, width, 512)
    cp_fac.wait()
    split_into(fac_st, ff_ref, nc, 512)
    pl.semaphore_wait(barrier, n - 1)
    send_parts(0, coarse, jnp.zeros((8, 128), F32))

    jr2 = bcast(weighted(jac_ref, r_ref))
    row_id = lax.broadcasted_iota(jnp.int32, (rows, ne), 0)
    inc_ref[...] = jnp.zeros_like(inc_ref)
    inc_ref[:, 0:ne] = ((row_id == edges_v[0:1, :]).astype(F32) - (row_id == edges_v[1:2, :]).astype(F32)).astype(BF16)
    row_id = lax.broadcasted_iota(jnp.int32, (rows, slots), 0)
    inc_ref[:, ne : ne + slots] = (row_id == ifr_v[...]).astype(F32).astype(BF16)
    inc_ref[:, ne + slots : ne + 2 * slots] = (-(row_id == snd_v[...]).astype(F32)).astype(BF16)
    used = (ne + 2 * slots) * loads
    if wide_e * loads > used:
        t_ref[used:, :] = jnp.zeros((wide_e * loads - used, 128), F32)

    tile, _ = take_parts(0)
    send_whole(0, tile, pack16(jr2))
    cp_blk.wait()
    cp_ifb.wait()
    split_into(stage_ref, bb_ref, stage_ref.shape[1], 512)
    gamma = take_whole(0, None)
    precondition(set_direction)

    for it in range(ITERS):
        @pl.loop(0, slots // 2)
        def _(k):
            halo_s[it, pl.ds(pl.multiple_of(k * 16, 16), 16), :] = jnp.where(
                low_half, v_ref[snd_s[0, 2 * k]], v_ref[snd_s[0, 2 * k + 1]]
            )

        cp_halo = pltpu.make_async_remote_copy(
            halo_s.at[it], halo_r.at[it], sh_sem.at[it], rh_sem.at[it], device_id={"sub": prv}, device_id_type=MESH
        )
        cp_halo.start()
        half = ne // 8
        acc = local_groups(0, half, jnp.zeros((loads, 256), F32))
        cp_halo.wait()

        def iface(g, acc):
            parts = []
            for a in range(2):
                x = halo_r[it, pl.ds(pl.multiple_of((2 * g + a) * 16, 16), 16), :]
                y = pltpu.roll(x, 64, 1)
                for b, there in enumerate((jnp.where(low_half, x, y), jnp.where(low_half, y, x))):
                    k = 4 * g + 2 * a + b
                    live = jnp.where(k < cnt_s[0], 1.0, 0.0).astype(F32)
                    parts.append((v_ref[ifr_s[0, k]] - there) * live)
            t, e = force(jnp.concatenate(parts, axis=0), lcols + 256 * g)
            put_force(ne + 4 * g, t)
            for a in range(2):
                frc_s[it, pl.ds(pl.multiple_of((2 * g + a) * 16, 16), 16), :] = jnp.where(
                    low_half, t[32 * a : 32 * a + 16], t[32 * a + 16 : 32 * a + 32]
                )
            return acc + e

        acc = lax.fori_loop(0, slots // 4, iface, acc)
        cp_frc = pltpu.make_async_remote_copy(
            frc_s.at[it], frc_r.at[it], sf_sem.at[it], rf_sem.at[it], device_id={"sub": nxt}, device_id_type=MESH
        )
        cp_frc.start()
        acc = local_groups(half, ne // 4, acc)
        energy = weighted(mass_ref, p_ref) + acc[:, :128] + acc[:, 128:]
        cp_frc.wait()

        @pl.loop(0, slots // 2)
        def _(k):
            x = frc_r[it, pl.ds(pl.multiple_of(k * 16, 16), 16), :]
            y = pltpu.roll(x, 64, 1)
            put_force(ne + slots + 2 * k, jnp.where(low_half, x, y))
            put_force(ne + slots + 2 * k + 1, jnp.where(low_half, y, x))

        @pl.loop(0, loads // 2)
        def _(k):
            f = jnp.concatenate([t_ref[pl.ds(2 * k + h, wide_e, stride=loads), :] for h in range(2)], axis=1).astype(BF16)
            o = dot(inc_ref[...], f)
            for h in range(2):
                a = o[:, 128 * h : 128 * h + 128]
                qrow_ref[pl.ds(2 * k + h, rows, stride=loads), :] = a + pltpu.roll(a, 64, 1)

        def image(i, o):
            cols = []
            for c in range(4):
                pair = qrow_ref[pl.ds(pl.multiple_of((8 * i + 2 * c) * 16, 32), 32), :]
                cols.append(jnp.where(low_half, pair[:16], pair[16:]))
            q = mass_ref[:, lanes(i, 512)] * p_ref[:, lanes(i, 512)] + jnp.concatenate(cols, axis=1)
            q_ref[:, lanes(i, 512)] = q
            return o + dot_t(stacked(q), bs_ref[:, lanes(i, 512)])

        coarse = fold(lax.fori_loop(0, width // 512, image, jnp.zeros((2 * loads, 128), F32)), loads)
        send_parts(it + 1, coarse, pack16(bcast(energy)))
        tile, energy = take_parts(it + 1)
        alpha = gamma / energy
        alpha4 = jnp.concatenate([alpha] * 4, axis=1)

        def update(i, s):
            r = r_ref[:, lanes(i, 512)] - alpha4 * q_ref[:, lanes(i, 512)]
            r_ref[:, lanes(i, 512)] = r
            v = jac_ref[:, lanes(i, 512)] * r * r
            return s + v[:, :128] + v[:, 128:256] + v[:, 256:384] + v[:, 384:]

        jr2 = bcast(lax.fori_loop(0, width // 512, update, jnp.zeros((loads, 128), F32)))
        send_whole(it + 1, tile, pack16(jr2))

        @pl.loop(0, width // 512)
        def _(i):
            step = alpha4 * p_ref[:, lanes(i, 512)]
            x_ref[:, lanes(i, 512)] = step if it == 0 else x_ref[:, lanes(i, 512)] + step

        new = take_whole(it + 1, alpha)
        if it + 1 < ITERS:
            beta4 = jnp.concatenate([new / gamma] * 4, axis=1)
            precondition(lambda i, z: set_direction(i, z + beta4 * p_ref[:, lanes(i, 512)]))
            gamma = new
        else:
            def finish(i, z):
                z_ref[:, lanes(i, 512)] = z
            precondition(finish)

    for phase in range(ITERS + 1):
        wait_all(rcv_a, phase, sa_sem)
        wait_all(rcv_b, phase, sb_sem)


def body(
    rhs,
    mass,
    jacobi,
    local_edges,
    local_blocks,
    if_rows,
    send_rows,
    if_count,
    if_blocks,
    coarse_basis,
    coarse_factor,
):
    n = lax.axis_size("sub")
    loads, width = rhs.shape
    ne = local_edges.shape[1]
    slots = if_rows.shape[0]
    nc = coarse_factor.shape[1]
    rows = width // 64
    wide_e = -(-(ne + 2 * slots) // 128) * 128
    cols = (ne + slots) * 64
    phases = ITERS + 1
    vmem = pl.BlockSpec(memory_space=pltpu.VMEM)
    smem = pl.BlockSpec(memory_space=pltpu.SMEM)
    hbm = pl.BlockSpec(memory_space=pl.ANY)
    dma = pltpu.SemaphoreType.DMA
    if_rows = if_rows.reshape(1, slots)
    send_rows = send_rows.reshape(1, slots)
    out = jax.ShapeDtypeStruct((loads, width), F32)
    return pl.pallas_call(
        functools.partial(kernel, n),
        out_shape=(out, out),
        in_specs=[vmem] * 2 + [smem] * 4 + [vmem] * 3 + [hbm] * 5,
        out_specs=(vmem, vmem),
        scratch_shapes=[
            pltpu.VMEM((loads, width), F32),
            pltpu.VMEM((loads, width), F32),
            pltpu.VMEM((loads, width), F32),
            pltpu.VMEM((rows, loads, 128), F32),
            pltpu.VMEM((rows * loads, 128), F32),
            pltpu.VMEM((wide_e * loads, 128), F32),
            pltpu.VMEM((rows, wide_e), BF16),
            pltpu.VMEM((64, cols), F32),
            pltpu.VMEM((64, width), F32),
            pltpu.VMEM((64, nc), F32),
            pltpu.VMEM((128, cols), BF16),
            pltpu.VMEM((128, width), BF16),
            pltpu.VMEM((128, nc), BF16),
            pltpu.VMEM((loads, nc), F32),
            pltpu.VMEM((8, 128), F32),
            pltpu.VMEM((phases, n, 16, 128), F32),
            pltpu.VMEM((phases, n, 16, 128), F32),
            pltpu.VMEM((phases, 16, 128), F32),
            pltpu.VMEM((phases, n, 16, 128), F32),
            pltpu.VMEM((ITERS, slots * 8, 128), F32),
            pltpu.VMEM((ITERS, slots * 8, 128), F32),
            pltpu.VMEM((ITERS, slots * 8, 128), F32),
            pltpu.VMEM((ITERS, slots * 8, 128), F32),
            dma((5,)),
            dma((phases,)),
            dma((phases,)),
            dma((phases,)),
            dma((phases,)),
            dma((ITERS,)),
            dma((ITERS,)),
            dma((ITERS,)),
            dma((ITERS,)),
        ],
        compiler_params=pltpu.CompilerParams(collective_id=0, has_side_effects=True, vmem_limit_bytes=56 * 2**20),
    )(
        mass.reshape(1, width),
        jacobi.reshape(1, width),
        local_edges,
        if_rows,
        send_rows,
        if_count,
        local_edges,
        if_rows,
        send_rows,
        rhs,
        local_blocks,
        if_blocks,
        coarse_basis,
        coarse_factor,
    )


def solution(mesh):
    in_specs = (
        P("groups", "sub"),
        P(("groups", "sub")),
        P(("groups", "sub")),
        P(None, ("groups", "sub")),
        P(None, ("groups", "sub")),
        P(("groups", "sub")),
        P(("groups", "sub")),
        P(("groups", "sub")),
        P(None, ("groups", "sub")),
        P(None, ("groups", "sub")),
        P(("groups", "sub"), None),
    )
    out_specs = (P("groups", "sub"), P("groups", "sub"))
    return jax.shard_map(body, mesh=mesh, in_specs=in_specs, out_specs=out_specs, check_vma=False)
```

time: 617 us -> 160 us (0.26); the launches traced: 608 us -> 160 us
  waiting for transfers between devices: 226 us -> 0 us
  matrix products: 163 us -> 0 us
  Pallas kernels: 0 us -> 154 us
  blocking collectives: 101 us -> 0 us
  local copies, waits for them, and re-layouts: 80 us -> 4.13 us
  other arithmetic: 14.4 us -> 0 us
  between operations: 15.2 us -> 1.29 us
  starting transfers between devices: 8.83 us -> 0 us
    psum x3 -> x0, waiting for transfers between devices: 226 us -> none  [precondition(): whole_w = lax.psum(partial_value, 'sub')]
    dot_general x26 -> x0, matrix products: 163 us -> none  [the longest x4 65.7 us: element_force(): return jnp.einsum('rej,kej->rek', strain, blocks, precision=HIGH)]
    pallas_call x0 -> x1, Pallas kernels: none -> 154 us  [body(): pl.pallas_call(functools.partial(kernel, n), out_shape=(out, out), in_spe...]
    psum x3 -> x0, blocking collectives: 101 us -> none  [the longest x2 67.2 us: load_sums(): return lax.psum(jnp.sum(left * right, axis=1), 'sub')]
    reshape x10 -> x0, local copies, waits for them, and re-layouts: 37.8 us -> none  [the longest x6 18.8 us: body(): field = direction.reshape(loads, rows, block)]
    gather x8 -> x0, local copies, waits for them, and re-layouts: 26.5 us -> none  [the longest x2 7.91 us: body(): field[:, local_edges[1]]]
    ppermute x5 -> x0, starting transfers between devices: 8.71 us -> none  [shifted(): return lax.ppermute(value, axis, pairs)]
    ppermute x2 -> x0, local copies, waits for them, and re-layouts: 6.21 us -> none  [shifted(): return lax.ppermute(value, axis, pairs)]
  transfers between devices with their start and end apart: 8 -> 0, of which waited for: 3 -> 0; matrix products, arithmetic and copies ran while one was open for 25% -> 0% of each run, Pallas kernels for 0% -> 0%
where the time goes in v1:
time: 160 us
  Pallas kernels  154 us (96%)
  local copies, waits for them, and re-layouts  4.13 us (3%)
    pallas_call x1, Pallas kernels, body(): pl.pallas_call(functools.partial(kernel, n), out_shape=(out, out), in_spe...  154 us
    unnamed x2, local copies, waits for them, and re-layouts  4.13 us

profile of v1, /device:TPU:0, one launch (start us, length us, event | category | flops | bytes accessed | tf_op | source)
XLA Modules:
  0.0 159.6 jit_solution(18031780341214767265)
XLA Ops:
  1.3 154.2 %shard_map.122 = (f32[16,12288]{1,0:T(8,128)}, f32[16,12288]{1,0:T(8,128)}) custom-call(f32[1,12288]{1,0:T(1,128)} %bitcast.4, f32[1,12288]{1,0:T(1,128)} %bitcast.5, s32[2,384]{1,0:T(2,128)} %edges_v.1, s32[1,32]{1,0:T(1,128)} %bitcast.6, s32[1,32]{1,0:T(1,128)} %bitcast.8, s32[1]{0:T(128)S(6)} %copy.15.cnt_s, s32[2,384]{1,0:T(2,128)} %edges_v.1, ...), custom_call_target="tpu_custom_call" | custom-call | tf_op jit(solution)/shard_map/pallas_call | solution.py:405
  155.4 2.1 %copy.16 = f32[16,12288]{1,0:T(8,128)} copy(f32[16,12288]{1,0:T(8,128)} %get-tuple-element.4) | data formatting | bytes 1572864
  157.5 2.1 %copy.17 = f32[16,12288]{1,0:T(8,128)} copy(f32[16,12288]{1,0:T(8,128)} %get-tuple-element.5) | data formatting | bytes 1572864

commit v2 on v1

--- a/solution.py
+++ b/solution.py
@@ -11,6 +11,8 @@
 F32 = jnp.float32
 BF16 = jnp.bfloat16
 MESH = pl.DeviceIdType.MESH
+GROUPS = 8
+UNROLL = 4
 
 
 def split(x):
@@ -130,20 +132,20 @@
         return jnp.broadcast_to(jnp.sum(s, axis=1, keepdims=True), (loads, 128))
 
     def split_into(src, dst, total, size):
-        @pl.loop(0, total // size)
+        @pl.loop(0, total // size, unroll=2)
         def _(i):
             dst[:, lanes(i, size)] = stacked(src[:, lanes(i, size)])
 
     def contract(src, mat, total, size):
         def step(i, o):
             return o + dot_t(stacked(src[:, lanes(i, size)]), mat[:, lanes(i, size)])
-        o = lax.fori_loop(0, total // size, step, jnp.zeros((2 * loads, 128), F32))
+        o = lax.fori_loop(0, total // size, step, jnp.zeros((2 * loads, 128), F32), unroll=2)
         return fold(o, loads)
 
     def send_parts(phase, coarse, scalars):
         lhs = stacked(coarse)
 
-        @pl.loop(0, nc // 512)
+        @pl.loop(0, nc // 512, unroll=2)
         def _(i):
             o = dot(lhs, ff_ref[:, lanes(i, 512)])
             o = o[:loads] + o[loads:]
@@ -168,7 +170,7 @@
 
     def take_parts(phase):
         wait_all(rcv_a, phase, ra_sem)
-        s = lax.fori_loop(0, n, lambda j, s: s + rcv_a[phase, j], jnp.zeros((16, 128), F32))
+        s = lax.fori_loop(0, n, lambda j, s: s + rcv_a[phase, j], jnp.zeros((16, 128), F32), unroll=8)
         return s[:8], unpack16(s[8:])
 
     def send_whole(phase, tile, scalars):
@@ -197,7 +199,7 @@
             w_ref[:, lanes(m, 128)] = w
             return norm + w * w, s + first[8:] + second[8:]
 
-        norm, s = lax.fori_loop(0, n // 2, step, (jnp.zeros((loads, 128), F32), jnp.zeros((8, 128), F32)))
+        norm, s = lax.fori_loop(0, n // 2, step, (jnp.zeros((loads, 128), F32), jnp.zeros((8, 128), F32)), unroll=4)
         return bcast(norm) + unpack16(s)
 
     def weighted(scale_ref, src):
@@ -205,12 +207,12 @@
             v = src[:, lanes(i, 512)]
             v = scale_ref[:, lanes(i, 512)] * v * v
             return s + v[:, :128] + v[:, 128:256] + v[:, 256:384] + v[:, 384:]
-        return lax.fori_loop(0, width // 512, step, jnp.zeros((loads, 128), F32))
+        return lax.fori_loop(0, width // 512, step, jnp.zeros((loads, 128), F32), unroll=UNROLL)
 
     def precondition(visit):
         lhs = stacked(contract(w_ref, ff_ref, nc, 512))
 
-        @pl.loop(0, width // 512)
+        @pl.loop(0, width // 512, unroll=UNROLL)
         def _(i):
             o = dot(lhs, bs_ref[:, lanes(i, 512)])
             visit(i, jac_ref[:, lanes(i, 512)] * r_ref[:, lanes(i, 512)] + o[:loads] + o[loads:])
@@ -229,21 +231,26 @@
             low_half64 if t.shape[0] == 64 else low_half, high, t - high
         )
 
-    def force(d, col):
-        b = bb_ref[:, pl.ds(pl.multiple_of(col, 256), 256)]
-        u = dot(stacked(d), b)
-        u = jnp.where(own_block, u[:64] + u[64:], 0.0)
-        t = fold(dot_t(stacked(u), b), 64)
-        u2 = u * u
-        return t, u2[0:16] + u2[16:32] + u2[32:48] + u2[48:64]
+    def force(diffs, cols):
+        mats = [bb_ref[:, pl.ds(pl.multiple_of(col, 256), 256)] for col in cols]
+        strains = [dot(stacked(d), b) for d, b in zip(diffs, mats)]
+        strains = [jnp.where(own_block, u[:64] + u[64:], 0.0) for u in strains]
+        forces = [fold(dot_t(stacked(u), b), 64) for u, b in zip(strains, mats)]
+        squares = [u * u for u in strains]
+        return forces, [u[0:16] + u[16:32] + u[32:48] + u[48:64] for u in squares]
 
     def local_groups(start, stop, acc):
-        def step(g, acc):
-            d = jnp.concatenate([v_ref[edges_s[0, 4 * g + k]] - v_ref[edges_s[1, 4 * g + k]] for k in range(4)], axis=0)
-            t, e = force(d, 256 * g)
-            put_force(4 * g, t)
-            return acc + e
-        return lax.fori_loop(start, stop, step, acc)
+        def step(i, acc):
+            groups = [GROUPS * i + b for b in range(GROUPS)]
+            diffs = []
+            for g in groups:
+                rows = [v_ref[edges_s[0, 4 * g + k]] - v_ref[edges_s[1, 4 * g + k]] for k in range(4)]
+                diffs.append(jnp.concatenate(rows, axis=0))
+            forces, energies = force(diffs, [256 * g for g in groups])
+            for g, t in zip(groups, forces):
+                put_force(4 * g, t)
+            return acc + sum(energies)
+        return lax.fori_loop(start // GROUPS, stop // GROUPS, step, acc)
 
     cp_rhs.wait()
     cp_basis.wait()
@@ -274,7 +281,7 @@
     precondition(set_direction)
 
     for it in range(ITERS):
-        @pl.loop(0, slots // 2)
+        @pl.loop(0, slots // 2, unroll=UNROLL)
         def _(k):
             halo_s[it, pl.ds(pl.multiple_of(k * 16, 16), 16), :] = jnp.where(
                 low_half, v_ref[snd_s[0, 2 * k]], v_ref[snd_s[0, 2 * k + 1]]
@@ -297,7 +304,7 @@
                     k = 4 * g + 2 * a + b
                     live = jnp.where(k < cnt_s[0], 1.0, 0.0).astype(F32)
                     parts.append((v_ref[ifr_s[0, k]] - there) * live)
-            t, e = force(jnp.concatenate(parts, axis=0), lcols + 256 * g)
+            (t,), (e,) = force([jnp.concatenate(parts, axis=0)], [lcols + 256 * g])
             put_force(ne + 4 * g, t)
             for a in range(2):
                 frc_s[it, pl.ds(pl.multiple_of((2 * g + a) * 16, 16), 16), :] = jnp.where(
@@ -305,7 +312,7 @@
                 )
             return acc + e
 
-        acc = lax.fori_loop(0, slots // 4, iface, acc)
+        acc = lax.fori_loop(0, slots // 4, iface, acc, unroll=4)
         cp_frc = pltpu.make_async_remote_copy(
             frc_s.at[it], frc_r.at[it], sf_sem.at[it], rf_sem.at[it], device_id={"sub": nxt}, device_id_type=MESH
         )
@@ -314,14 +321,14 @@
         energy = weighted(mass_ref, p_ref) + acc[:, :128] + acc[:, 128:]
         cp_frc.wait()
 
-        @pl.loop(0, slots // 2)
+        @pl.loop(0, slots // 2, unroll=UNROLL)
         def _(k):
             x = frc_r[it, pl.ds(pl.multiple_of(k * 16, 16), 16), :]
             y = pltpu.roll(x, 64, 1)
             put_force(ne + slots + 2 * k, jnp.where(low_half, x, y))
             put_force(ne + slots + 2 * k + 1, jnp.where(low_half, y, x))
 
-        @pl.loop(0, loads // 2)
+        @pl.loop(0, loads // 2, unroll=2)
         def _(k):
             f = jnp.concatenate([t_ref[pl.ds(2 * k + h, wide_e, stride=loads), :] for h in range(2)], axis=1).astype(BF16)
             o = dot(inc_ref[...], f)
@@ -338,7 +345,7 @@
             q_ref[:, lanes(i, 512)] = q
             return o + dot_t(stacked(q), bs_ref[:, lanes(i, 512)])
 
-        coarse = fold(lax.fori_loop(0, width // 512, image, jnp.zeros((2 * loads, 128), F32)), loads)
+        coarse = fold(lax.fori_loop(0, width // 512, image, jnp.zeros((2 * loads, 128), F32), unroll=UNROLL), loads)
         send_parts(it + 1, coarse, pack16(bcast(energy)))
         tile, energy = take_parts(it + 1)
         alpha = gamma / energy
@@ -350,10 +357,10 @@
             v = jac_ref[:, lanes(i, 512)] * r * r
             return s + v[:, :128] + v[:, 128:256] + v[:, 256:384] + v[:, 384:]
 
-        jr2 = bcast(lax.fori_loop(0, width // 512, update, jnp.zeros((loads, 128), F32)))
+        jr2 = bcast(lax.fori_loop(0, width // 512, update, jnp.zeros((loads, 128), F32), unroll=UNROLL))
         send_whole(it + 1, tile, pack16(jr2))
 
-        @pl.loop(0, width // 512)
+        @pl.loop(0, width // 512, unroll=UNROLL)
         def _(i):
             step = alpha4 * p_ref[:, lanes(i, 512)]
             x_ref[:, lanes(i, 512)] = step if it == 0 else x_ref[:, lanes(i, 512)] + step

time: 160 us -> 80.6 us (0.50)
  Pallas kernels: 154 us -> 74.9 us
    pallas_call x1, Pallas kernels: 154 us -> 74.9 us  [body(): pl.pallas_call(functools.partial(kernel, n), out_shape=(out, out), in_spe...]
where the time goes in v2:
time: 80.6 us; the launch traced here: 80.3 us
  Pallas kernels  74.9 us (93%)
  local copies, waits for them, and re-layouts  4.13 us (5%)
  between operations  1.29 us (2%)
    pallas_call x1, Pallas kernels, body(): pl.pallas_call(functools.partial(kernel, n), out_shape=(out, out), in_spe...  74.9 us
    unnamed x2, local copies, waits for them, and re-layouts  4.13 us

profile of v2, /device:TPU:0, one launch (start us, length us, event | category | flops | bytes accessed | tf_op | source)
XLA Modules:
  0.0 80.3 jit_solution(16789687734618365292)
XLA Ops:
  1.3 74.9 %shard_map.122 = (f32[16,12288]{1,0:T(8,128)}, f32[16,12288]{1,0:T(8,128)}) custom-call(f32[1,12288]{1,0:T(1,128)} %bitcast.4, f32[1,12288]{1,0:T(1,128)} %bitcast.5, s32[2,384]{1,0:T(2,128)} %edges_v.1, s32[1,32]{1,0:T(1,128)} %bitcast.6, s32[1,32]{1,0:T(1,128)} %bitcast.8, s32[1]{0:T(128)S(6)} %copy.15.cnt_s, s32[2,384]{1,0:T(2,128)} %edges_v.1, ...), custom_call_target="tpu_custom_call" | custom-call | tf_op jit(solution)/shard_map/pallas_call | solution.py:412
  76.2 2.1 %copy.16 = f32[16,12288]{1,0:T(8,128)} copy(f32[16,12288]{1,0:T(8,128)} %get-tuple-element.4) | data formatting | bytes 1572864
  78.2 2.1 %copy.17 = f32[16,12288]{1,0:T(8,128)} copy(f32[16,12288]{1,0:T(8,128)} %get-tuple-element.5) | data formatting | bytes 1572864

commit v3 on v2

--- a/solution.py
+++ b/solution.py
@@ -12,6 +12,7 @@
 BF16 = jnp.bfloat16
 MESH = pl.DeviceIdType.MESH
 GROUPS = 8
+PIECES = 4
 UNROLL = 4
 
 
@@ -70,11 +71,12 @@
     bs_ref,
     ff_ref,
     w_ref,
-    pw_ref,
     msg_a,
     rcv_a,
     msg_b,
     rcv_b,
+    msg_c,
+    rcv_c,
     halo_s,
     halo_r,
     frc_s,
@@ -84,6 +86,8 @@
     ra_sem,
     sb_sem,
     rb_sem,
+    sc_sem,
+    rc_sem,
     sh_sem,
     rh_sem,
     sf_sem,
@@ -115,18 +119,12 @@
         pl.semaphore_signal(barrier, inc=1, device_id={"sub": lax.rem(me + k, n)}, device_id_type=MESH)
 
     low_half = lax.broadcasted_iota(jnp.int32, (loads, 128), 1) < 64
-    low_half8 = lax.broadcasted_iota(jnp.int32, (8, 128), 1) < 64
+    diagonal = lax.broadcasted_iota(jnp.int32, (loads, 128), 0) == lax.broadcasted_iota(jnp.int32, (loads, 128), 1)
     low_half64 = lax.broadcasted_iota(jnp.int32, (64, 128), 1) < 64
     own_block = (lax.broadcasted_iota(jnp.int32, (64, 256), 0) >> 4) == (lax.broadcasted_iota(jnp.int32, (64, 256), 1) >> 6)
 
     def lanes(i, size):
         return pl.ds(pl.multiple_of(i * size, size), size)
-
-    def pack16(s):
-        return jnp.where(low_half8, s[:8], s[8:])
-
-    def unpack16(t):
-        return jnp.concatenate([jnp.broadcast_to(t[:, 0:1], (8, 128)), jnp.broadcast_to(t[:, 64:65], (8, 128))], axis=0)
 
     def bcast(s):
         return jnp.broadcast_to(jnp.sum(s, axis=1, keepdims=True), (loads, 128))
@@ -142,7 +140,7 @@
         o = lax.fori_loop(0, total // size, step, jnp.zeros((2 * loads, 128), F32), unroll=2)
         return fold(o, loads)
 
-    def send_parts(phase, coarse, scalars):
+    def send_parts(phase, coarse):
         lhs = stacked(coarse)
 
         @pl.loop(0, nc // 512, unroll=2)
@@ -151,8 +149,7 @@
             o = o[:loads] + o[loads:]
             for c in range(4):
                 for h in range(2):
-                    msg_a[phase, 8 * i + 2 * c + h, 0:8] = o[8 * h : 8 * h + 8, 128 * c : 128 * c + 128]
-                    msg_a[phase, 8 * i + 2 * c + h, 8:16] = scalars
+                    msg_a[phase, 8 * i + 2 * c + h] = o[8 * h : 8 * h + 8, 128 * c : 128 * c + 128]
 
         rcv_a[phase, me] = msg_a[phase, me]
 
@@ -168,15 +165,11 @@
         part = buf.at[phase, pl.ds(0, n - 1)]
         pltpu.make_async_copy(part, part, sem.at[phase]).wait()
 
-    def take_parts(phase):
+    def pass_on(phase):
         wait_all(rcv_a, phase, ra_sem)
-        s = lax.fori_loop(0, n, lambda j, s: s + rcv_a[phase, j], jnp.zeros((16, 128), F32), unroll=8)
-        return s[:8], unpack16(s[8:])
-
-    def send_whole(phase, tile, scalars):
-        both = jnp.concatenate([tile, scalars], axis=0)
-        msg_b[phase] = both
-        rcv_b[phase, me] = both
+        tile = lax.fori_loop(0, n, lambda j, s: s + rcv_a[phase, j], jnp.zeros((8, 128), F32), unroll=8)
+        msg_b[phase] = tile
+        rcv_b[phase, me] = tile
 
         @pl.loop(1, n)
         def _(k):
@@ -189,18 +182,32 @@
     def take_whole(phase, alpha):
         wait_all(rcv_b, phase, rb_sem)
 
-        def step(m, carry):
-            norm, s = carry
-            first = rcv_b[phase, 2 * m]
-            second = rcv_b[phase, 2 * m + 1]
-            w = jnp.concatenate([first[:8], second[:8]], axis=0)
+        def step(m, norm):
+            w = jnp.concatenate([rcv_b[phase, 2 * m], rcv_b[phase, 2 * m + 1]], axis=0)
             if alpha is not None:
                 w = w_ref[:, lanes(m, 128)] - alpha * w
             w_ref[:, lanes(m, 128)] = w
-            return norm + w * w, s + first[8:] + second[8:]
-
-        norm, s = lax.fori_loop(0, n // 2, step, (jnp.zeros((loads, 128), F32), jnp.zeros((8, 128), F32)), unroll=4)
-        return bcast(norm) + unpack16(s)
+            return norm + w * w
+
+        return bcast(lax.fori_loop(0, n // 2, step, jnp.zeros((loads, 128), F32), unroll=4))
+
+    def send_scalars(phase, s):
+        line = jnp.sum(jnp.where(diagonal, bcast(s), 0.0), axis=0, keepdims=True)
+        msg_c[phase] = line
+        rcv_c[phase, me] = line
+
+        @pl.loop(1, n)
+        def _(k):
+            to = lax.rem(me + k, n)
+            pltpu.make_async_remote_copy(
+                msg_c.at[phase], rcv_c.at[phase, me], sc_sem.at[phase], rc_sem.at[phase],
+                device_id={"sub": to}, device_id_type=MESH,
+            ).start()
+
+    def take_scalars(phase):
+        wait_all(rcv_c, phase, rc_sem)
+        line = lax.fori_loop(0, n, lambda j, s: s + rcv_c[phase, j], jnp.zeros((1, 128), F32), unroll=8)
+        return bcast(jnp.where(diagonal, jnp.broadcast_to(line, (loads, 128)), 0.0))
 
     def weighted(scale_ref, src):
         def step(i, s):
@@ -259,9 +266,8 @@
     cp_fac.wait()
     split_into(fac_st, ff_ref, nc, 512)
     pl.semaphore_wait(barrier, n - 1)
-    send_parts(0, coarse, jnp.zeros((8, 128), F32))
-
-    jr2 = bcast(weighted(jac_ref, r_ref))
+    send_parts(0, coarse)
+    send_scalars(0, weighted(jac_ref, r_ref))
     row_id = lax.broadcasted_iota(jnp.int32, (rows, ne), 0)
     inc_ref[...] = jnp.zeros_like(inc_ref)
     inc_ref[:, 0:ne] = ((row_id == edges_v[0:1, :]).astype(F32) - (row_id == edges_v[1:2, :]).astype(F32)).astype(BF16)
@@ -272,54 +278,66 @@
     if wide_e * loads > used:
         t_ref[used:, :] = jnp.zeros((wide_e * loads - used, 128), F32)
 
-    tile, _ = take_parts(0)
-    send_whole(0, tile, pack16(jr2))
+    pass_on(0)
     cp_blk.wait()
     cp_ifb.wait()
     split_into(stage_ref, bb_ref, stage_ref.shape[1], 512)
-    gamma = take_whole(0, None)
+    gamma = take_whole(0, None) + take_scalars(0)
     precondition(set_direction)
 
     for it in range(ITERS):
-        @pl.loop(0, slots // 2, unroll=UNROLL)
-        def _(k):
-            halo_s[it, pl.ds(pl.multiple_of(k * 16, 16), 16), :] = jnp.where(
-                low_half, v_ref[snd_s[0, 2 * k]], v_ref[snd_s[0, 2 * k + 1]]
-            )
-
-        cp_halo = pltpu.make_async_remote_copy(
-            halo_s.at[it], halo_r.at[it], sh_sem.at[it], rh_sem.at[it], device_id={"sub": prv}, device_id_type=MESH
-        )
-        cp_halo.start()
+        piece = slots * 8 // PIECES
+        halos = []
+        for c in range(PIECES):
+            for k in range(c * slots // 2 // PIECES, (c + 1) * slots // 2 // PIECES):
+                halo_s[it, 16 * k : 16 * k + 16, :] = jnp.where(
+                    low_half, v_ref[snd_s[0, 2 * k]], v_ref[snd_s[0, 2 * k + 1]]
+                )
+            part = pl.ds(c * piece, piece)
+            halos.append(pltpu.make_async_remote_copy(
+                halo_s.at[it, part], halo_r.at[it, part], sh_sem.at[it, c], rh_sem.at[it, c],
+                device_id={"sub": prv}, device_id_type=MESH,
+            ))
+            halos[-1].start()
         half = ne // 8
         acc = local_groups(0, half, jnp.zeros((loads, 256), F32))
-        cp_halo.wait()
-
-        def iface(g, acc):
-            parts = []
-            for a in range(2):
-                x = halo_r[it, pl.ds(pl.multiple_of((2 * g + a) * 16, 16), 16), :]
-                y = pltpu.roll(x, 64, 1)
-                for b, there in enumerate((jnp.where(low_half, x, y), jnp.where(low_half, y, x))):
-                    k = 4 * g + 2 * a + b
-                    live = jnp.where(k < cnt_s[0], 1.0, 0.0).astype(F32)
-                    parts.append((v_ref[ifr_s[0, k]] - there) * live)
-            (t,), (e,) = force([jnp.concatenate(parts, axis=0)], [lcols + 256 * g])
-            put_force(ne + 4 * g, t)
-            for a in range(2):
-                frc_s[it, pl.ds(pl.multiple_of((2 * g + a) * 16, 16), 16), :] = jnp.where(
-                    low_half, t[32 * a : 32 * a + 16], t[32 * a + 16 : 32 * a + 32]
-                )
-            return acc + e
-
-        acc = lax.fori_loop(0, slots // 4, iface, acc, unroll=4)
-        cp_frc = pltpu.make_async_remote_copy(
-            frc_s.at[it], frc_r.at[it], sf_sem.at[it], rf_sem.at[it], device_id={"sub": nxt}, device_id_type=MESH
-        )
-        cp_frc.start()
+
+        def interface(first, count):
+            diffs = []
+            for g in range(first, first + count):
+                parts = []
+                for a in range(2):
+                    x = halo_r[it, 32 * g + 16 * a : 32 * g + 16 * a + 16, :]
+                    y = pltpu.roll(x, 64, 1)
+                    for b, there in enumerate((jnp.where(low_half, x, y), jnp.where(low_half, y, x))):
+                        k = 4 * g + 2 * a + b
+                        live = jnp.where(k < cnt_s[0], 1.0, 0.0).astype(F32)
+                        parts.append((v_ref[ifr_s[0, k]] - there) * live)
+                diffs.append(jnp.concatenate(parts, axis=0))
+            forces, energies = force(diffs, [lcols + 256 * g for g in range(first, first + count)])
+            for g, t in zip(range(first, first + count), forces):
+                put_force(ne + 4 * g, t)
+                for a in range(2):
+                    frc_s[it, 32 * g + 16 * a : 32 * g + 16 * a + 16, :] = jnp.where(
+                        low_half, t[32 * a : 32 * a + 16], t[32 * a + 16 : 32 * a + 32]
+                    )
+            return sum(energies)
+
+        replies = []
+        for c in range(PIECES):
+            halos[c].wait()
+            acc = acc + interface(c * slots // 4 // PIECES, slots // 4 // PIECES)
+            part = pl.ds(c * piece, piece)
+            replies.append(pltpu.make_async_remote_copy(
+                frc_s.at[it, part], frc_r.at[it, part], sf_sem.at[it, c], rf_sem.at[it, c],
+                device_id={"sub": nxt}, device_id_type=MESH,
+            ))
+            replies[-1].start()
         acc = local_groups(half, ne // 4, acc)
         energy = weighted(mass_ref, p_ref) + acc[:, :128] + acc[:, 128:]
-        cp_frc.wait()
+        send_scalars(2 * it + 1, energy)
+        for reply in replies:
+            reply.wait()
 
         @pl.loop(0, slots // 2, unroll=UNROLL)
         def _(k):
@@ -346,9 +364,8 @@
             return o + dot_t(stacked(q), bs_ref[:, lanes(i, 512)])
 
         coarse = fold(lax.fori_loop(0, width // 512, image, jnp.zeros((2 * loads, 128), F32), unroll=UNROLL), loads)
-        send_parts(it + 1, coarse, pack16(bcast(energy)))
-        tile, energy = take_parts(it + 1)
-        alpha = gamma / energy
+        send_parts(it + 1, coarse)
+        alpha = gamma / take_scalars(2 * it + 1)
         alpha4 = jnp.concatenate([alpha] * 4, axis=1)
 
         def update(i, s):
@@ -357,16 +374,19 @@
             v = jac_ref[:, lanes(i, 512)] * r * r
             return s + v[:, :128] + v[:, 128:256] + v[:, 256:384] + v[:, 384:]
 
-        jr2 = bcast(lax.fori_loop(0, width // 512, update, jnp.zeros((loads, 128), F32), unroll=UNROLL))
-        send_whole(it + 1, tile, pack16(jr2))
+        jr2 = lax.fori_loop(0, width // 512, update, jnp.zeros((loads, 128), F32), unroll=UNROLL)
+        if it + 1 < ITERS:
+            send_scalars(2 * it + 2, jr2)
+        pass_on(it + 1)
 
         @pl.loop(0, width // 512, unroll=UNROLL)
         def _(i):
             step = alpha4 * p_ref[:, lanes(i, 512)]
             x_ref[:, lanes(i, 512)] = step if it == 0 else x_ref[:, lanes(i, 512)] + step
 
-        new = take_whole(it + 1, alpha)
+        norm = take_whole(it + 1, alpha)
         if it + 1 < ITERS:
+            new = norm + take_scalars(2 * it + 2)
             beta4 = jnp.concatenate([new / gamma] * 4, axis=1)
             precondition(lambda i, z: set_direction(i, z + beta4 * p_ref[:, lanes(i, 512)]))
             gamma = new
@@ -378,6 +398,8 @@
     for phase in range(ITERS + 1):
         wait_all(rcv_a, phase, sa_sem)
         wait_all(rcv_b, phase, sb_sem)
+    for phase in range(2 * ITERS):
+        wait_all(rcv_c, phase, sc_sem)
 
 
 def body(
@@ -429,11 +451,12 @@
             pltpu.VMEM((128, width), BF16),
             pltpu.VMEM((128, nc), BF16),
             pltpu.VMEM((loads, nc), F32),
-            pltpu.VMEM((8, 128), F32),
-            pltpu.VMEM((phases, n, 16, 128), F32),
-            pltpu.VMEM((phases, n, 16, 128), F32),
-            pltpu.VMEM((phases, 16, 128), F32),
-            pltpu.VMEM((phases, n, 16, 128), F32),
+            pltpu.VMEM((phases, n, 8, 128), F32),
+            pltpu.VMEM((phases, n, 8, 128), F32),
+            pltpu.VMEM((phases, 8, 128), F32),
+            pltpu.VMEM((phases, n, 8, 128), F32),
+            pltpu.VMEM((2 * ITERS, 1, 128), F32),
+            pltpu.VMEM((2 * ITERS, n, 1, 128), F32),
             pltpu.VMEM((ITERS, slots * 8, 128), F32),
             pltpu.VMEM((ITERS, slots * 8, 128), F32),
             pltpu.VMEM((ITERS, slots * 8, 128), F32),
@@ -443,10 +466,12 @@
             dma((phases,)),
             dma((phases,)),
             dma((phases,)),
-            dma((ITERS,)),
-            dma((ITERS,)),
-            dma((ITERS,)),
-            dma((ITERS,)),
+            dma((2 * ITERS,)),
+            dma((2 * ITERS,)),
+            dma((ITERS, PIECES)),
+            dma((ITERS, PIECES)),
+            dma((ITERS, PIECES)),
+            dma((ITERS, PIECES)),
         ],
         compiler_params=pltpu.CompilerParams(collective_id=0, has_side_effects=True, vmem_limit_bytes=56 * 2**20),
     )(

time: 80.6 us -> 75.6 us (0.938)
  Pallas kernels: 74.9 us -> 69.9 us
    pallas_call x1, Pallas kernels: 74.9 us -> 69.9 us  [body(): pl.pallas_call(functools.partial(kernel, n), out_shape=(out, out), in_spe...]
where the time goes in v3:
time: 75.6 us; the launch traced here: 75.3 us
  Pallas kernels  69.9 us (92%)
  local copies, waits for them, and re-layouts  4.13 us (5%)
  between operations  1.29 us (2%)
    pallas_call x1, Pallas kernels, body(): pl.pallas_call(functools.partial(kernel, n), out_shape=(out, out), in_spe...  69.9 us
    unnamed x2, local copies, waits for them, and re-layouts  4.13 us

profile of v3, /device:TPU:0, one launch (start us, length us, event | category | flops | bytes accessed | tf_op | source)
XLA Modules:
  0.0 75.3 jit_solution(3223535739851075200)
XLA Ops:
  1.3 69.9 %shard_map.122 = (f32[16,12288]{1,0:T(8,128)}, f32[16,12288]{1,0:T(8,128)}) custom-call(f32[1,12288]{1,0:T(1,128)} %bitcast.4, f32[1,12288]{1,0:T(1,128)} %bitcast.5, s32[2,384]{1,0:T(2,128)} %edges_v.1, s32[1,32]{1,0:T(1,128)} %bitcast.6, s32[1,32]{1,0:T(1,128)} %bitcast.8, s32[1]{0:T(128)S(6)} %copy.15.cnt_s, s32[2,384]{1,0:T(2,128)} %edges_v.1, ...), custom_call_target="tpu_custom_call" | custom-call | tf_op jit(solution)/shard_map/pallas_call | solution.py:434
  71.2 2.1 %copy.16 = f32[16,12288]{1,0:T(8,128)} copy(f32[16,12288]{1,0:T(8,128)} %get-tuple-element.4) | data formatting | bytes 1572864
  73.2 2.1 %copy.17 = f32[16,12288]{1,0:T(8,128)} copy(f32[16,12288]{1,0:T(8,128)} %get-tuple-element.5) | data formatting | bytes 1572864

commit v4 on v3

--- a/solution.py
+++ b/solution.py
@@ -12,7 +12,7 @@
 BF16 = jnp.bfloat16
 MESH = pl.DeviceIdType.MESH
 GROUPS = 8
-PIECES = 4
+PIECES = 2
 UNROLL = 4
 
 
@@ -402,6 +402,11 @@
         wait_all(rcv_c, phase, sc_sem)
 
 
+def hand_over(x_ref, z_ref, x_out, z_out):
+    x_out[...] = x_ref[...]
+    z_out[...] = z_ref[...]
+
+
 def body(
     rhs,
     mass,
@@ -431,7 +436,7 @@
     if_rows = if_rows.reshape(1, slots)
     send_rows = send_rows.reshape(1, slots)
     out = jax.ShapeDtypeStruct((loads, width), F32)
-    return pl.pallas_call(
+    result = pl.pallas_call(
         functools.partial(kernel, n),
         out_shape=(out, out),
         in_specs=[vmem] * 2 + [smem] * 4 + [vmem] * 3 + [hbm] * 5,
@@ -490,6 +495,13 @@
         coarse_basis,
         coarse_factor,
     )
+    return pl.pallas_call(
+        hand_over,
+        grid=(2,),
+        out_shape=(out, out),
+        in_specs=[pl.BlockSpec((loads, width // 2), lambda i: (0, i))] * 2,
+        out_specs=[pl.BlockSpec((loads, width // 2), lambda i: (0, i))] * 2,
+    )(*result)
 
 
 def solution(mesh):

time: 75.6 us -> 73.4 us (0.971)
  local copies, waits for them, and re-layouts: 4.13 us -> 0 us
  Pallas kernels: 69.9 us -> 71.9 us
    unnamed x2 -> x0, local copies, waits for them, and re-layouts: 4.13 us -> none
    pallas_call x0 -> x1, Pallas kernels: none -> 2.31 us  [body(): pl.pallas_call(hand_over, grid=(2,), out_shape=(out, out), in_specs=[pl.B...]
where the time goes in v4:
time: 73.4 us; the launch traced here: 73.2 us
  Pallas kernels  71.9 us (98%)
  between operations  1.29 us (2%)
    pallas_call x1, Pallas kernels, body(): pl.pallas_call(functools.partial(kernel, n), out_shape=(out, out), in_spe...  69.6 us
    pallas_call x1, Pallas kernels, body(): pl.pallas_call(hand_over, grid=(2,), out_shape=(out, out), in_specs=[pl.B...  2.31 us

profile of v4, /device:TPU:0, one launch (start us, length us, event | category | flops | bytes accessed | tf_op | source)
XLA Modules:
  0.0 73.2 jit_solution(5486406336302612314)
XLA Ops:
  1.3 69.6 %shard_map.122 = (f32[16,12288]{1,0:T(8,128)}, f32[16,12288]{1,0:T(8,128)}) custom-call(f32[1,12288]{1,0:T(1,128)} %bitcast.4, f32[1,12288]{1,0:T(1,128)} %bitcast.5, s32[2,384]{1,0:T(2,128)} %edges_v.1, s32[1,32]{1,0:T(1,128)} %bitcast.6, s32[1,32]{1,0:T(1,128)} %bitcast.8, s32[1]{0:T(128)S(6)} %copy.13.cnt_s, s32[2,384]{1,0:T(2,128)} %edges_v.1, ...), custom_call_target="tpu_custom_call" | custom-call | tf_op jit(solution)/shard_map/pallas_call | solution.py:439
  70.8 2.3 %shard_map.123 = (f32[16,12288]{1,0:T(8,128)}, f32[16,12288]{1,0:T(8,128)}) custom-call(f32[16,12288]{1,0:T(8,128)} %get-tuple-element.4.x_ref, f32[16,12288]{1,0:T(8,128)} %get-tuple-element.5.z_ref), custom_call_target="tpu_custom_call" | custom-call | tf_op jit(solution)/shard_map/pallas_call | solution.py:498
